TPU v7x, 256 devices: a whole 4x4x8 slice. The times are simulated.
256 devices in a mesh: sample: 16 (over x, y), landmark: 16 (over z, core).
Axes of the slice: x: 4, y: 4, z: 8, core: 2. Of those that a mesh axis runs over, the one named last changes fastest.
Arguments:
- embeddings: float32 [65536, 512], P('sample')
- landmark_index: int32 [8192], P('landmark'), may hold values from 0 to 65535, as said below
- cluster_weights: float32 [8192, 256], P('landmark'), may hold values from -6 to 6
Outputs:
- scores: float32 [65536, 256], P(('sample', 'landmark'))
Inputs may be any that keep to these rules, and one draw needn't show every extreme that they name: `landmark_index`: 8192 distinct sample indices; 0 and 65535 are always among them.
All inputs are finite; a program needn't handle non-finite values.
Results may differ from a plain program's by a relative error of at most 0.00018.
Values sent between devices are 32-bit elements; how exact they have to be, the bound alone decides.
A program may use at most 128 MiB of HBM per device.

v0:
```python
import jax
import jax.numpy as jnp
from jax import lax
from jax.sharding import PartitionSpec as P

kernel_gamma = 2.0


def make_logits(row_block, landmarks):
    row_sq = jnp.sum(row_block * row_block, axis=1)
    land_sq = jnp.sum(landmarks * landmarks, axis=1)
    inner_prod = jnp.dot(
        row_block, landmarks.T, precision=lax.Precision.HIGHEST, preferred_element_type=jnp.float32
    )
    return (2.0 * inner_prod - row_sq[:, None] - land_sq[None, :]) * kernel_gamma


def shards(embeddings, landmark_index, cluster_weights):
    row_count = embeddings.shape[0]
    sample_pos = lax.axis_index("sample")
    land_pos = lax.axis_index("landmark")
    offsets = landmark_index - sample_pos * row_count
    owned_mask = (offsets >= 0) & (offsets < row_count)
    picked = jnp.take(embeddings, jnp.clip(offsets, 0, row_count - 1), axis=0)
    picked = jnp.where(owned_mask[:, None], picked, 0.0)
    landmarks = lax.psum(picked, "sample")
    own_count = row_count // lax.axis_size("landmark")
    own_rows = lax.dynamic_slice_in_dim(embeddings, land_pos * own_count, own_count, 0)
    old_max = jnp.full((own_count,), -jnp.inf, jnp.float32)
    old_mass = jnp.zeros((own_count,), jnp.float32)
    old_weighted = jnp.zeros((own_count, cluster_weights.shape[1]), jnp.float32)
    land_piece = lax.all_gather(landmarks, "landmark", axis=0, tiled=True)
    weight_piece = lax.all_gather(cluster_weights, "landmark", axis=0, tiled=True)
    logits = make_logits(own_rows, land_piece)
    new_max = jnp.max(logits, axis=1)
    rescale = jnp.exp(old_max - new_max)
    kernel = jnp.exp(logits - new_max[:, None])
    new_mass = old_mass * rescale + jnp.sum(kernel, axis=1)
    new_weighted = old_weighted * rescale[:, None] + jnp.dot(
        kernel, weight_piece, precision=lax.Precision.HIGHEST, preferred_element_type=jnp.float32
    )
    return new_weighted / new_mass[:, None]


def solution(mesh):
    return jax.shard_map(
        shards,
        mesh=mesh,
        in_specs=(P("sample", None), P("landmark"), P("landmark", None)),
        out_specs=P(("sample", "landmark"), None),
        check_vma=False,
    )
```

profile of v0, /device:TPU:1, one launch (start us, length us, event | category | flops | bytes accessed | tf_op | source)
XLA Modules:
  0.0 289.3 jit_solution(314359011119413678)
XLA Ops:
  6.5 0.0 all-reduce.2.cloned.1.call-start
  6.5 0.7 compare_and_fusion
  7.2 5.4 %gather_fusion = f32[512,512]{1,0:T(8,128)S(1)} fusion(f32[4096,512]{1,0:T(8,128)} %param.3, s32[1024]{0:T(1024)S(1)} %pad_clamp_fusion), kind=kCustom, calls=%fused_computation | custom fusion | bytes 2099200 | tf_op jit(solution)/shard_map/jit(_take)/gather | solution.py:24
  12.7 1.2 select_select_fusion
  13.9 0.0 all-reduce.2.cloned.1.call-update
  13.9 0.0 all-gather.3.cloned.1.call-start
  13.9 99.6 %all-reduce.2.cloned.1.call-done = f32[512,512]{1,0:T(8,128)} async-done(((f32[512,512]{1,0:T(8,128)}), f32[512,512]{1,0:T(8,128)}) %all-reduce.2.cloned.1.call-update) | async-done | bytes 1048592 | tf_op jit(solution)/shard_map/psum | solution.py:26
  113.5 0.0 all-gather.3.cloned.1.call-update
  113.5 0.0 all-gather.5.cloned.1.call-start
  113.6 0.7 all-gather.5.cloned.1.call-update
  114.3 1.2 multiply_reduce_fusion.1
  115.4 96.5 %all-gather.3.cloned.1.call-done = f32[8192,512]{1,0:T(8,128)} async-done(((f32[512,512]{1,0:T(8,128)}), f32[8192,512]{1,0:T(8,128)}) %all-gather.3.cloned.1.call-update) | async-done | bytes 16777232 | tf_op jit(solution)/shard_map/all_gather | solution.py:32
  211.9 7.0 %multiply_reduce_fusion = f32[8192]{0:T(1024)S(1)} fusion(f32[8192,512]{1,0:T(8,128)} %all-gather.3.cloned.1.call-done), kind=kLoop, calls=%fused_computation.1 | loop fusion | flops 8380416 | bytes 16809984 | tf_op jit(solution)/shard_map/reduce_sum | solution.py:11
  218.9 17.7 %fusion.11 = (f32[256]{0:T(256)S(1)}, f32[256,8192]{1,0:T(8,128)S(1)}) fusion(f32[8192]{0:T(1024)S(1)} %multiply_reduce_fusion, f32[256]{0:T(256)S(1)} %multiply_reduce_fusion.1, f32[8192,512]{1,0:T(8,128)} %all-gather.3.cloned.1.call-done, f32[4096,512]{1,0:T(8,128)} %param.3, s32[]{:T(128)S(6)} %select_n.16), kind=kOutput, calls=%fused_computation.22 | convolution fusion | flops 12895387648 | bytes 25724932 | tf_op jit(solution)/shard_map/dot_general | solution.py:12
  236.6 0.0 copy-start
  236.6 3.2 %copy-done = f32[256,8192]{1,0:T(8,128)} copy-done((f32[256,8192]{1,0:T(8,128)}, f32[256,8192]{1,0:T(8,128)S(1)}, u32[]{:S(2)}) %copy-start) | copy-done | bytes 8388632
  239.8 1.3 fusion.3
  241.2 27.1 %all-gather.5.cloned.1.call-done = f32[8192,256]{1,0:T(8,128)} async-done(((f32[512,256]{1,0:T(8,128)}), f32[8192,256]{1,0:T(8,128)}) %all-gather.5.cloned.1.call-update) | async-done | bytes 8388624 | tf_op jit(solution)/shard_map/all_gather | solution.py:33
  268.2 14.5 %fusion.7 = f32[256,256]{1,0:T(8,128)} fusion(f32[8192,256]{1,0:T(8,128)} %all-gather.5.cloned.1.call-done, f32[256,8192]{1,0:T(8,128)} %copy-done, f32[256]{0:T(256)S(1)} %get-tuple-element.10, f32[256]{0:T(256)S(1)} %get-tuple-element.9, f32[256]{0:T(256)S(1)} %get-tuple-element.8), kind=kOutput, calls=%fused_computation.11 | convolution fusion | flops 6444679168 | bytes 17042432 | tf_op jit(solution)/shard_map/dot_general | solution.py:39
  (2 shorter events, 0.0 us)
Async XLA Ops:
  6.5 107.0 %all-reduce.2.cloned.1.call-start = ((), (), s32[]{:S(2)}) async-start(), calls=%async_computation | async-start | bytes 2097152 | tf_op jit(solution)/shard_map/psum | solution.py:26
  13.9 198.1 %all-gather.3.cloned.1.call-start = ((), (), s32[]{:S(2)}) async-start(), calls=%async_computation.1 | async-start | bytes 17825792 | tf_op jit(solution)/shard_map/all_gather | solution.py:32
  113.5 154.7 %all-gather.5.cloned.1.call-start = ((), (), s32[]{:S(2)}) async-start(), calls=%async_computation.2 | async-start | bytes 8912896 | tf_op jit(solution)/shard_map/all_gather | solution.py:33
  236.6 3.2 %copy-start = (f32[256,8192]{1,0:T(8,128)}, f32[256,8192]{1,0:T(8,128)S(1)}, u32[]{:S(2)}) copy-start(f32[256,8192]{1,0:T(8,128)S(1)} %get-tuple-element.11) | copy-start | bytes 25165828
Sparse Core Ops, SparseCore 0:
  14.0 99.4 all-reduce.1
  115.3 96.5 all-gather.2
  213.8 54.4 all-gather.4
where the time goes:
time: 290 us; the launch traced here: 289 us
  waiting for transfers between devices  224 us (77%)
  matrix products  32.2 us (11%)
  between operations  13.1 us (5%)
  other arithmetic  11.4 us (4%)
  local copies, waits for them, and re-layouts  8.62 us (3%)
    psum x1, waiting for transfers between devices, shards(): landmarks = lax.psum(picked, 'sample')  99.6 us
    all_gather x1, waiting for transfers between devices, shards(): land_piece = lax.all_gather(landmarks, 'landmark', axis=0, tiled=True)  96.5 us
    all_gather x1, waiting for transfers between devices, shards(): lax.all_gather(cluster_weights, 'landmark', axis=0, tiled=True)  27.1 us
    dot_general x1, matrix products, make_logits(): jnp.dot(row_block, landmarks.T, precision=lax.Precision.HIGHEST, preferre...  17.7 us
    dot_general x1, matrix products, shards(): jnp.dot(kernel, weight_piece, precision=lax.Precision.HIGHEST, preferred_...  14.5 us
    reduce_sum x1, other arithmetic, make_logits(): land_sq = jnp.sum(landmarks * landmarks, axis=1)  6.96 us
  transfers between devices with their start and end apart: 3, of which 3 were waited for; matrix products, arithmetic and copies ran while one was open for 9% of the time, Pallas kernels for 0%

commit v1 on v0

v1 whole, which is shorter than its diff:
```python
import jax
import jax.numpy as jnp
from jax import lax
from jax.sharding import PartitionSpec as P

kernel_gamma = 2.0


def dot3(a, b):
    return jnp.dot(a, b, precision=lax.Precision.HIGH, preferred_element_type=jnp.float32)


def shards(embeddings, landmark_index, cluster_weights):
    row_count = embeddings.shape[0]
    sample_pos = lax.axis_index("sample")
    offsets = landmark_index - sample_pos * row_count
    owned_mask = (offsets >= 0) & (offsets < row_count)
    picked = jnp.take(embeddings, jnp.clip(offsets, 0, row_count - 1), axis=0)
    picked = jnp.where(owned_mask[:, None], picked, 0.0)
    landmarks = lax.psum(picked, "sample")
    row_sq = jnp.sum(embeddings * embeddings, axis=1)
    land_sq = jnp.sum(landmarks * landmarks, axis=1)
    inner = dot3(embeddings, landmarks.T)
    logits = (2.0 * inner - row_sq[:, None] - land_sq[None, :]) * kernel_gamma
    top = lax.pmax(jnp.max(logits, axis=1), "landmark")
    kernel = jnp.exp(logits - top[:, None])
    mass = lax.psum_scatter(jnp.sum(kernel, axis=1), "landmark", tiled=True)
    weighted = lax.psum_scatter(dot3(kernel, cluster_weights), "landmark", tiled=True)
    return weighted / mass[:, None]


def solution(mesh):
    return jax.shard_map(
        shards,
        mesh=mesh,
        in_specs=(P("sample", None), P("landmark"), P("landmark", None)),
        out_specs=P(("sample", "landmark"), None),
        check_vma=False,
    )
```

time: 290 us -> 257 us (0.89)
  waiting for transfers between devices: 224 us -> 105 us
  blocking collectives: 0 us -> 91.2 us
  matrix products: 32.2 us -> 24 us
    all_gather x2 -> x0, waiting for transfers between devices: 124 us -> none  [the longest x1 96.5 us: shards(): land_piece = lax.all_gather(landmarks, 'landmark', axis=0, tiled=True)]
    unnamed x0 -> x1, blocking collectives: none -> 45.8 us
    pmax x0 -> x1, blocking collectives: none -> 45.4 us  [shards(): top = lax.pmax(jnp.max(logits, axis=1), 'landmark')]
    reduce_scatter x0 -> x1, waiting for transfers between devices: none -> 9.41 us  [shards(): lax.psum_scatter(dot3(kernel, cluster_weights), 'landmark', tiled=True)]
    dot_general x2, matrix products: 32.2 us -> 24 us  [dot3(): jnp.dot(a, b, precision=lax.Precision.HIGH, preferred_element_type=jnp.fl...]
    psum x1, waiting for transfers between devices: 99.6 us -> 95.6 us  [shards(): landmarks = lax.psum(picked, 'sample')]
  transfers between devices with their start and end apart: 3 -> 2, of which waited for: 3 -> 2; matrix products, arithmetic and copies ran while one was open for 9% -> 4% of each run, Pallas kernels for 0% -> 0%
where the time goes in v1:
time: 257 us; the launch traced here: 254 us
  waiting for transfers between devices  105 us (41%)
  blocking collectives  91.2 us (35%)
  matrix products  24 us (9%)
  between operations  14.1 us (5%)
  other arithmetic  13.6 us (5%)
  local copies, waits for them, and re-layouts  6.08 us (2%)
    psum x1, waiting for transfers between devices, shards(): landmarks = lax.psum(picked, 'sample')  95.6 us
    unnamed x1, blocking collectives  45.8 us
    pmax x1, blocking collectives, shards(): top = lax.pmax(jnp.max(logits, axis=1), 'landmark')  45.4 us
    dot_general x2, matrix products, dot3(): jnp.dot(a, b, precision=lax.Precision.HIGH, preferred_element_type=jnp.fl...  24 us
    reduce_scatter x1, waiting for transfers between devices, shards(): lax.psum_scatter(dot3(kernel, cluster_weights), 'landmark', tiled=True)  9.41 us
    gather x1, local copies, waits for them, and re-layouts, shards(): picked = jnp.take(embeddings, jnp.clip(offsets, 0, row_count - 1), axis=0)  5.41 us
  transfers between devices with their start and end apart: 2, of which 2 were waited for; matrix products, arithmetic and copies ran while one was open for 4% of the time, Pallas kernels for 0%

profile of v1, /device:TPU:1, one launch (start us, length us, event | category | flops | bytes accessed | tf_op | source)
XLA Modules:
  0.0 254.0 jit_solution(5110716832233641124)
XLA Ops:
  6.5 0.0 copy-start
  6.5 0.0 all-reduce.3.cloned.1.call-start
  6.5 0.7 compare_and_fusion
  7.3 5.4 %gather_fusion = f32[512,512]{1,0:T(8,128)S(1)} fusion(f32[4096,512]{1,0:T(8,128)} %param.3, s32[1024]{0:T(1024)S(1)} %pad_clamp_fusion), kind=kCustom, calls=%fused_computation | custom fusion | bytes 2099200 | tf_op jit(solution)/shard_map/jit(_take)/gather | solution.py:18
  12.7 1.2 select_select_fusion
  13.9 0.0 all-reduce.3.cloned.1.call-update
  13.9 0.0 reduce-scatter.2.cloned.1.call-start
  14.0 4.0 %multiply_reduce_fusion = f32[4096]{0:T(1024)S(1)} fusion(f32[4096,512]{1,0:T(8,128)} %param.3), kind=kLoop, calls=%fused_computation.3 | loop fusion | flops 4190208 | bytes 8404992 | tf_op jit(solution)/shard_map/reduce_sum | solution.py:21
  18.0 95.6 %all-reduce.3.cloned.1.call-done = f32[512,512]{1,0:T(8,128)} async-done(((f32[512,512]{1,0:T(8,128)}), f32[512,512]{1,0:T(8,128)}) %all-reduce.3.cloned.1.call-update) | async-done | bytes 1048592 | tf_op jit(solution)/shard_map/psum | solution.py:20
  113.6 1.4 multiply_reduce_fusion.1
  114.9 11.9 %fusion.3 = (f32[4096]{0:T(1024)S(1)}, f32[512,4096]{1,0:T(8,128)}) fusion(f32[512]{0:T(512)S(1)} %multiply_reduce_fusion.1, f32[4096]{0:T(1024)S(1)} %multiply_reduce_fusion, f32[512,512]{1,0:T(8,128)} %all-reduce.3.cloned.1.call-done, f32[4096,512]{1,0:T(8,128)} %param.3), kind=kOutput, calls=%fused_computation.14 | convolution fusion | flops 6452932608 | bytes 17860608 | tf_op jit(solution)/shard_map/dot_general | solution.py:10
  126.8 45.4 %pmax.7 = f32[4096]{0:T(1024)S(1)} all-reduce(f32[4096]{0:T(1024)S(1)} %get-tuple-element.8), channel_id=1, replica_groups=mesh['sample'=16,'landmark'=16] {'landmark'}, use_global_device_ids=true, to_apply=%region_4.5 | all-reduce | flops 4096 | bytes 32768 | tf_op jit(solution)/shard_map/pmax | solution.py:25
  172.2 0.0 copy-done
  172.3 0.0 copy-start.1
  172.3 12.1 %fusion.1 = f32[4096,256]{1,0:T(8,128)} fusion(f32[512,256]{1,0:T(8,128)S(1)} %copy-done, f32[512,4096]{1,0:T(8,128)} %get-tuple-element.9, f32[4096]{0:T(1024)S(1)} %pmax.7), kind=kOutput, calls=%fused_computation.5 | convolution fusion | flops 3223322624 | bytes 13123584 | tf_op jit(solution)/shard_map/dot_general | solution.py:10
  184.3 0.0 reduce-scatter.2.cloned.1.call-update
  184.4 0.0 copy-done.1
  184.4 0.6 dynamic-slice
  185.6 4.5 %fusion = f32[4096]{0:T(1024)S(1)} fusion(f32[512,4096]{1,0:T(8,128)} %get-tuple-element.9, f32[4096]{0:T(1024)S(1)} %pmax.7), kind=kLoop, calls=%fused_computation.4 | loop fusion | flops 4190208 | bytes 8421376 | tf_op jit(solution)/shard_map/reduce_sum | solution.py:27
  190.2 45.8 %all-reduce = f32[4096]{0:T(1024)S(1)} all-reduce(f32[4096]{0:T(1024)S(1)} %fusion), channel_id=3, replica_groups=mesh['sample'=16,'landmark'=16] {'landmark'}, use_global_device_ids=true, to_apply=%region_7.8.clone | all-reduce | flops 4096 | bytes 32768
  235.9 0.1 dynamic-slice.1
  236.0 9.4 %reduce-scatter.2.cloned.1.call-done = f32[256,256]{1,0:T(8,128)} async-done(((f32[4096,256]{1,0:T(8,128)}), f32[256,256]{1,0:T(8,128)}) %reduce-scatter.2.cloned.1.call-update) | async-done | bytes 262160 | tf_op jit(solution)/shard_map/reduce_scatter | solution.py:28
  245.4 1.8 broadcast_divide_fusion
  (1 shorter events, 0.0 us)
Async XLA Ops:
  6.5 165.7 %copy-start = (f32[512,256]{1,0:T(8,128)S(1)}, f32[512,256]{1,0:T(8,128)}, u32[]{:S(2)}) copy-start(f32[512,256]{1,0:T(8,128)} %param.5) | copy-start | bytes 1572868
  6.5 107.0 %all-reduce.3.cloned.1.call-start = ((), (), s32[]{:S(2)}) async-start(), calls=%async_computation.1 | async-start | bytes 2097152 | tf_op jit(solution)/shard_map/psum | solution.py:20
  13.9 231.5 %reduce-scatter.2.cloned.1.call-start = ((), (), s32[]{:S(2)}) async-start(), calls=%async_computation.2 | async-start | bytes 4456448 | tf_op jit(solution)/shard_map/reduce_scatter | solution.py:28
  172.3 12.1 %copy-start.1 = (u32[256]{0:T(256)S(1)}, u32[256]{0:T(256)}, u32[]{:S(2)}) copy-start(u32[256]{0:T(256)} %constant.34) | copy-start | bytes 3076
Sparse Core Ops, SparseCore 0:
  14.1 99.4 all-reduce.2
  184.5 60.8 reduce-scatter.1

commit v2 on v1

v2 whole, which is shorter than its diff:
```python
import jax
import jax.numpy as jnp
from jax import lax
from jax.experimental import pallas as pl
from jax.experimental.pallas import tpu as pltpu
from jax.sharding import PartitionSpec as P

MESH = pl.DeviceIdType.MESH
F32 = jnp.float32
BF16 = jnp.bfloat16

D = 512
C = 256
ROWS = 4096
OWN = 512
PAIR = 2 * OWN
RING = 8
CHUNK = 256
HALF = CHUNK // 2
STREAMS = 8
R = OWN // STREAMS
MSG = C + 8
LOADS = 8


def split(a):
    hi = a.astype(BF16)
    return hi, (a - hi.astype(F32)).astype(BF16)


def kernel(
    emb_hbm, idx_ref, w_hbm, out_ref,
    emb, pick, land, buf0, buf1, buf2, buf3, acc1, acc2, acc3,
    wts, ww, ll, lsq2, xx, xsq2, sent, got,
    load_sem, w_sem, send_sem, recv_sem, sib_send, sib_recv, ws_send, ws_recv, ring_send, ring_recv,
):
    sample = lax.axis_index("sample")
    mark = lax.axis_index("landmark")
    x, y = sample // 4, sample % 4
    z, core = mark // 2, mark % 2

    partners = [
        ((x + 1 - 2 * (x % 2)) * 4 + y, mark),
        ((3 - x) * 4 + y, mark),
        (x * 4 + y + 1 - 2 * (y % 2), mark),
        (x * 4 + 3 - y, mark),
    ]
    bits = [(x % 2 + x // 2) % 2, x // 2, (y % 2 + y // 2) % 2, y // 2]
    sibling = (sample, z * 2 + 1 - core)
    above = (sample, ((z + 1) % RING) * 2 + core)
    below = (sample, ((z + RING - 1) % RING) * 2 + core)

    loads = []
    for i in range(LOADS):
        part = pl.ds(i * (ROWS // LOADS), ROWS // LOADS)
        load = pltpu.make_async_copy(emb_hbm.at[part], emb.at[part], load_sem.at[i])
        load.start()
        loads.append(load)
    own_w = pl.ds(pl.multiple_of(core * OWN, OWN), OWN)
    w_load = pltpu.make_async_copy(w_hbm, wts.at[own_w], w_sem)
    w_load.start()

    barrier = pltpu.get_barrier_semaphore()
    for other in partners + [sibling, above, below]:
        pl.semaphore_signal(barrier, inc=1, device_id=other, device_id_type=MESH)
    pl.semaphore_wait(barrier, 7)

    w_load.wait()
    w_send = pltpu.make_async_remote_copy(
        wts.at[own_w], wts.at[own_w], ws_send, ws_recv, device_id=sibling, device_id_type=MESH
    )
    w_send.start()

    for load in loads:
        load.wait()

    first = sample * ROWS

    def pick_rows(i, carry):
        for u in range(16):
            row = i * 16 + u
            place = idx_ref[row] - first
            owned = jnp.logical_and(place >= 0, place < ROWS)
            found = emb[pl.ds(jnp.clip(place, 0, ROWS - 1), 1), :]
            pick[pl.ds(row, 1), :] = jnp.where(owned, found, 0.0)
        return carry

    def prepare(t):
        up = ((z + 2 * RING - 1 - t) % RING * 2 + core) * CHUNK
        down = ((z + 1 + t) % RING * 2 + core) * CHUNK + HALF
        for side, start in enumerate((up, down)):
            rows = emb[pl.ds(pl.multiple_of(start, HALF), HALF), :]
            hi, lo = split(4.0 * rows)
            here = pl.ds(side * HALF, HALF)
            xx[t, here, 0:D] = hi
            xx[t, here, D : 2 * D] = lo
            xx[t, here, 2 * D :] = hi
            sq = rows * rows
            sq = (sq[:, 0:128] + sq[:, 128:256]) + (sq[:, 256:384] + sq[:, 384:512])
            xsq2[t, :, side * HALF : (side + 1) * HALF] = 2.0 * jnp.sum(sq.T, axis=0, keepdims=True)

    def prepare_landmarks(start, count):
        here = pl.ds(pl.multiple_of(start, 16), count)
        rows = land[here, :]
        hi, lo = split(rows)
        ll[here, 0:D] = hi
        ll[here, D : 2 * D] = hi
        ll[here, 2 * D :] = lo
        lsq2[here, :] = jnp.broadcast_to(2.0 * jnp.sum(rows * rows, axis=1, keepdims=True), (count, 128))

    def prepare_weights():
        for g in range(PAIR // 256):
            hi, lo = split(wts[g * 256 : (g + 1) * 256, :].T)
            ww[0:C, g * 256 : (g + 1) * 256] = hi
            ww[C:, g * 256 : (g + 1) * 256] = lo

    lax.fori_loop(0, OWN // 16, pick_rows, 0)

    copies = []

    def send(step, j, src, dst, dim):
        copy = pltpu.make_async_remote_copy(
            src, dst, send_sem.at[step, j], recv_sem.at[step, j],
            device_id=partners[dim], device_id_type=MESH,
        )
        copy.start()
        copies.append(copy)
        return copy

    def rows_at(start, count):
        return pl.ds(pl.multiple_of(start, 8), count)

    flight = []
    for j in range(STREAMS):
        b0 = bits[j % 4]
        flight.append(send(0, j, pick.at[rows_at(j * R + (1 - b0) * (R // 2), R // 2)], buf0.at[j], j % 4))
    prepare(0)
    prepare(1)
    for j in range(STREAMS):
        b0, b1 = bits[j % 4], bits[(j + 1) % 4]
        flight[j].wait_recv()
        acc1[j] = pick[rows_at(j * R + b0 * (R // 2), R // 2), :] + buf0[j]
        flight[j] = send(1, j, acc1.at[j, rows_at((1 - b1) * (R // 4), R // 4)], buf1.at[j], (j + 1) % 4)
    prepare(2)
    prepare(3)
    for j in range(STREAMS):
        b1 = bits[(j + 1) % 4]
        flight[j].wait_recv()
        acc2[j] = acc1[j, rows_at(b1 * (R // 4), R // 4), :] + buf1[j]
        flight[j] = send(2, j, acc2.at[j], buf2.at[j], (j + 2) % 4)
    prepare(4)
    prepare(5)
    for j in range(STREAMS):
        flight[j].wait_recv()
        acc3[j] = acc2[j] + buf2[j]
        flight[j] = send(3, j, acc3.at[j], buf3.at[j], (j + 3) % 4)
    prepare(6)
    prepare(7)
    base = core * OWN
    for j in range(STREAMS):
        b0, b1 = bits[j % 4], bits[(j + 1) % 4]
        here = rows_at(base + j * R + b0 * (R // 2) + b1 * (R // 4), R // 4)
        flight[j].wait_recv()
        land[here, :] = acc3[j] + buf3[j]
        flight[j] = send(4, j, land.at[here], land.at[here], (j + 1) % 4)
    w_send.wait()
    prepare_weights()
    shares = []

    def share(which, start, count):
        here = rows_at(start, count)
        copy = pltpu.make_async_remote_copy(
            land.at[here], land.at[here], sib_send.at[which], sib_recv.at[which],
            device_id=sibling, device_id_type=MESH,
        )
        copy.start()
        shares.append(copy)

    for j in range(STREAMS):
        b0 = bits[j % 4]
        start = base + j * R + b0 * (R // 2)
        flight[j].wait_recv()
        flight[j] = send(5, j, land.at[rows_at(start, R // 2)], land.at[rows_at(start, R // 2)], j % 4)
        share(j, start, R // 2)
    for j in range(STREAMS):
        b0 = bits[j % 4]
        flight[j].wait_recv()
        share(STREAMS + j, base + j * R + (1 - b0) * (R // 2), R // 2)
    for j in range(STREAMS):
        prepare_landmarks(base + j * R, R)
    for copy in shares:
        copy.wait_recv()
    for j in range(STREAMS):
        prepare_landmarks((1 - core) * OWN + j * R, R)

    def ring_copy(t, side):
        return pltpu.make_async_remote_copy(
            sent.at[t, side], got.at[t, side], ring_send.at[t, side], ring_recv.at[t, side],
            device_id=above if side == 0 else below, device_id_type=MESH,
        )

    for t in range(RING):
        inner = lax.dot_general(ll[...], xx[t], (((1,), (1,)), ((), ())), preferred_element_type=F32)
        row = xsq2[t]
        both = lsq2[...]
        logits = inner - jnp.concatenate([both, both], axis=1) - row
        top = jnp.max(logits, axis=0, keepdims=True)
        weight = jnp.exp(logits - top)
        mass = jnp.sum(weight, axis=0, keepdims=True)
        hi, lo = split(weight)
        part = jnp.dot(ww[...], hi, preferred_element_type=F32)
        part = part[:C] + part[C:] + jnp.dot(ww[0:C, :], lo, preferred_element_type=F32)
        for side in range(2):
            lanes = slice(side * HALF, (side + 1) * HALF)
            p, m, s = part[:, lanes], top[:, lanes], mass[:, lanes]
            if t > 0:
                ring_copy(t - 1, side).wait_recv()
                m_in = got[t - 1, side, C : C + 1, :]
                s_in = got[t - 1, side, C + 1 : C + 2, :]
                m_new = jnp.maximum(m, m_in)
                mine, theirs = jnp.exp(m - m_new), jnp.exp(m_in - m_new)
                p = p * mine + got[t - 1, side, 0:C, :] * theirs
                m, s = m_new, s * mine + s_in * theirs
            if t < RING - 1:
                sent[t, side, 0:C, :] = p
                sent[t, side, C : C + 1, :] = m
                sent[t, side, C + 1 : C + 2, :] = s
                sent[t, side, C + 2 :, :] = jnp.zeros((MSG - C - 2, HALF), F32)
                ring_copy(t, side).start()
            else:
                out_ref[side * HALF : (side + 1) * HALF, :] = (p / s).T

    for copy in copies + shares:
        copy.wait_send()
    for t in range(RING - 1):
        for side in range(2):
            ring_copy(t, side).wait_send()


def shards(embeddings, landmark_index, cluster_weights):
    vmem = lambda *shape, dtype=F32: pltpu.VMEM(shape, dtype)
    dma = lambda *shape: pltpu.SemaphoreType.DMA(shape)
    return pl.pallas_call(
        kernel,
        out_shape=jax.ShapeDtypeStruct((CHUNK, C), F32),
        in_specs=[
            pl.BlockSpec(memory_space=pl.ANY),
            pl.BlockSpec(memory_space=pltpu.SMEM),
            pl.BlockSpec(memory_space=pl.ANY),
        ],
        out_specs=pl.BlockSpec(memory_space=pltpu.VMEM),
        scratch_shapes=[
            vmem(ROWS, D),
            vmem(OWN, D),
            vmem(PAIR, D),
            vmem(STREAMS, R // 2, D),
            vmem(STREAMS, R // 4, D),
            vmem(STREAMS, R // 4, D),
            vmem(STREAMS, R // 4, D),
            vmem(STREAMS, R // 2, D),
            vmem(STREAMS, R // 4, D),
            vmem(STREAMS, R // 4, D),
            vmem(PAIR, C),
            vmem(2 * C, PAIR, dtype=BF16),
            vmem(PAIR, 3 * D, dtype=BF16),
            vmem(PAIR, 128),
            vmem(RING, CHUNK, 3 * D, dtype=BF16),
            vmem(RING, 1, CHUNK),
            vmem(RING - 1, 2, MSG, HALF),
            vmem(RING - 1, 2, MSG, HALF),
            dma(LOADS),
            pltpu.SemaphoreType.DMA,
            dma(6, STREAMS),
            dma(6, STREAMS),
            dma(2 * STREAMS),
            dma(2 * STREAMS),
            pltpu.SemaphoreType.DMA,
            pltpu.SemaphoreType.DMA,
            dma(RING - 1, 2),
            dma(RING - 1, 2),
        ],
        compiler_params=pltpu.CompilerParams(
            collective_id=0, has_side_effects=True, vmem_limit_bytes=56 * 2**20
        ),
    )(embeddings, landmark_index, cluster_weights)


def solution(mesh):
    return jax.shard_map(
        shards,
        mesh=mesh,
        in_specs=(P("sample", None), P("landmark"), P("landmark", None)),
        out_specs=P(("sample", "landmark"), None),
        check_vma=False,
    )
```

time: 257 us -> 76.7 us (0.30)
  the two profiles are of different devices: /device:TPU:1 before, /device:TPU:64 now
where the time goes in v2:
time: 76.7 us; the launch traced here: 76.6 us
  Pallas kernels  74.9 us (98%)
  local copies, waits for them, and re-layouts  1.67 us (2%)
    pallas_call x1, Pallas kernels, shards(): pl.pallas_call(kernel, out_shape=jax.ShapeDtypeStruct((CHUNK, C), F32), i...  74.9 us
    unnamed x1, local copies, waits for them, and re-layouts  1.67 us

profile of v2, /device:TPU:64, one launch (start us, length us, event | category | flops | bytes accessed | tf_op | source)
XLA Modules:
  0.0 76.6 jit_solution(8488658118967661504)
XLA Ops:
  0.0 74.9 %shard_map.37 = f32[256,256]{1,0:T(8,128)} custom-call(f32[4096,512]{1,0:T(8,128)} %emb_hbm.1, s32[512]{0:T(512)} %idx_ref.1, f32[512,256]{1,0:T(8,128)} %w_hbm.1), custom_call_target="tpu_custom_call" | custom-call | tf_op jit(solution)/shard_map/pallas_call | solution.py:243
  74.9 1.7 %copy.5 = f32[256,256]{1,0:T(8,128)} copy(f32[256,256]{1,0:T(8,128)} %shard_map.37) | data formatting | bytes 524288

commit v3 on v2

v3 whole, which is shorter than its diff:
```python
import jax
import jax.numpy as jnp
from jax import lax
from jax.experimental import pallas as pl
from jax.experimental.pallas import tpu as pltpu
from jax.sharding import PartitionSpec as P

MESH = pl.DeviceIdType.MESH
F32 = jnp.float32
BF16 = jnp.bfloat16

D = 512
C = 256
ROWS = 4096
OWN = 512
PAIR = 2 * OWN
RING = 8
CHUNK = 256
HALF = CHUNK // 2
STREAMS = 8
R = OWN // STREAMS
HEAD = 8
MSG = HEAD + C
SUBS = 4
PART = C // SUBS
BLOCKS = 4
BLOCK = PAIR // BLOCKS
LOADS = 8


def split(a):
    hi = a.astype(BF16)
    return hi, (a - hi.astype(F32)).astype(BF16)


def kernel(
    emb_hbm, idx_ref, w_hbm, out_ref,
    emb, pick, land, buf0, buf1, buf2, buf3, acc1, acc2, acc3,
    wts, ww, ll, lsq2, xx, xsq2, dots0, dots1, held0, held1, sent, got,
    load_sem, w_sem, send_sem, recv_sem, sib_send, sib_recv, ws_send, ws_recv, ring_send, ring_recv,
):
    sample = lax.axis_index("sample")
    mark = lax.axis_index("landmark")
    x, y = sample // 4, sample % 4
    z, core = mark // 2, mark % 2

    partners = [
        ((x + 1 - 2 * (x % 2)) * 4 + y, mark),
        ((3 - x) * 4 + y, mark),
        (x * 4 + y + 1 - 2 * (y % 2), mark),
        (x * 4 + 3 - y, mark),
    ]
    bits = [(x % 2 + x // 2) % 2, x // 2, (y % 2 + y // 2) % 2, y // 2]
    sibling = (sample, z * 2 + 1 - core)
    above = (sample, ((z + 1) % RING) * 2 + core)
    below = (sample, ((z + RING - 1) % RING) * 2 + core)

    barrier = pltpu.get_barrier_semaphore()
    for other in partners + [sibling, above, below]:
        pl.semaphore_signal(barrier, inc=1, device_id=other, device_id_type=MESH)

    loads = []
    for i in range(LOADS):
        part = pl.ds(i * (ROWS // LOADS), ROWS // LOADS)
        load = pltpu.make_async_copy(emb_hbm.at[part], emb.at[part], load_sem.at[i])
        load.start()
        loads.append(load)
    own_w = pl.ds(pl.multiple_of(core * OWN, OWN), OWN)
    w_load = pltpu.make_async_copy(w_hbm, wts.at[own_w], w_sem)
    w_load.start()

    first = sample * ROWS

    def pick_rows(start, count):
        def some(i, carry):
            for u in range(16):
                row = start + i * 16 + u
                place = idx_ref[row] - first
                owned = jnp.logical_and(place >= 0, place < ROWS)
                found = emb[pl.ds(jnp.clip(place, 0, ROWS - 1), 1), :]
                pick[pl.ds(row, 1), :] = jnp.where(owned, found, 0.0)
            return carry

        lax.fori_loop(0, count // 16, some, 0)

    def prepare(t):
        up = ((z + 2 * RING - 1 - t) % RING * 2 + core) * CHUNK
        down = ((z + 1 + t) % RING * 2 + core) * CHUNK + HALF
        for side, start in enumerate((up, down)):
            rows = emb[pl.ds(pl.multiple_of(start, HALF), HALF), :]
            hi, lo = split(4.0 * rows)
            here = pl.ds(side * HALF, HALF)
            xx[t, here, 0:D] = hi
            xx[t, here, D : 2 * D] = lo
            xx[t, here, 2 * D :] = hi
            sq = rows * rows
            sq = (sq[:, 0:128] + sq[:, 128:256]) + (sq[:, 256:384] + sq[:, 384:512])
            xsq2[t, :, side * HALF : (side + 1) * HALF] = 2.0 * jnp.sum(sq.T, axis=0, keepdims=True)

    base = core * OWN
    other_base = (1 - core) * OWN

    def rows_at(start, count):
        return pl.ds(pl.multiple_of(start, 8), count)

    def block_rows(block, j):
        b0 = bits[j % 4]
        late = block // 2
        half = b0 + late - 2 * b0 * late
        return (base if block % 2 == 0 else other_base) + j * R + half * (R // 2)

    def prepare_landmarks(block, j):
        rows = land[rows_at(block_rows(block, j), R // 2), :]
        hi, lo = split(rows)
        here = pl.ds(block * BLOCK + j * (R // 2), R // 2)
        ll[here, 0:D] = hi
        ll[here, D : 2 * D] = hi
        ll[here, 2 * D :] = lo
        lsq2[here, :] = jnp.broadcast_to(2.0 * jnp.sum(rows * rows, axis=1, keepdims=True), (R // 2, 128))

    def prepare_weights(block):
        rows = [wts[rows_at(block_rows(block, j), R // 2), :] for j in range(STREAMS)]
        hi, lo = split(jnp.concatenate(rows, axis=0).T)
        here = slice(block * BLOCK, (block + 1) * BLOCK)
        ww[0:C, here] = hi
        ww[C:, here] = lo

    copies = []

    def send(step, j, src, dst, dim):
        copy = pltpu.make_async_remote_copy(
            src, dst, send_sem.at[step, j], recv_sem.at[step, j],
            device_id=partners[dim], device_id_type=MESH,
        )
        copy.start()
        copies.append(copy)
        return copy

    for load in loads:
        load.wait()
    for j in range(STREAMS):
        pick_rows(j * R + (1 - bits[j % 4]) * (R // 2), R // 2)
    for t in range(RING):
        prepare(t)
    w_load.wait()
    prepare_weights(0)
    prepare_weights(2)

    pl.semaphore_wait(barrier, 7)
    flight = []
    for j in range(STREAMS):
        b0 = bits[j % 4]
        flight.append(send(0, j, pick.at[rows_at(j * R + (1 - b0) * (R // 2), R // 2)], buf0.at[j], j % 4))
    w_send = pltpu.make_async_remote_copy(
        wts.at[own_w], wts.at[own_w], ws_send, ws_recv, device_id=sibling, device_id_type=MESH
    )
    w_send.start()
    for j in range(STREAMS):
        pick_rows(j * R + bits[j % 4] * (R // 2), R // 2)
    for j in range(STREAMS):
        b0, b1 = bits[j % 4], bits[(j + 1) % 4]
        flight[j].wait_recv()
        acc1[j] = pick[rows_at(j * R + b0 * (R // 2), R // 2), :] + buf0[j]
        flight[j] = send(1, j, acc1.at[j, rows_at((1 - b1) * (R // 4), R // 4)], buf1.at[j], (j + 1) % 4)
    for j in range(STREAMS):
        b1 = bits[(j + 1) % 4]
        flight[j].wait_recv()
        acc2[j] = acc1[j, rows_at(b1 * (R // 4), R // 4), :] + buf1[j]
        flight[j] = send(2, j, acc2.at[j], buf2.at[j], (j + 2) % 4)
    w_send.wait()
    prepare_weights(1)
    for j in range(STREAMS):
        flight[j].wait_recv()
        acc3[j] = acc2[j] + buf2[j]
        flight[j] = send(3, j, acc3.at[j], buf3.at[j], (j + 3) % 4)
    prepare_weights(3)
    for j in range(STREAMS):
        b0, b1 = bits[j % 4], bits[(j + 1) % 4]
        here = rows_at(base + j * R + b0 * (R // 2) + b1 * (R // 4), R // 4)
        flight[j].wait_recv()
        land[here, :] = acc3[j] + buf3[j]
        flight[j] = send(4, j, land.at[here], land.at[here], (j + 1) % 4)
    shares = []

    def share(which, start, count):
        here = rows_at(start, count)
        copy = pltpu.make_async_remote_copy(
            land.at[here], land.at[here], sib_send.at[which], sib_recv.at[which],
            device_id=sibling, device_id_type=MESH,
        )
        copy.start()
        shares.append(copy)

    for j in range(STREAMS):
        here = rows_at(block_rows(0, j), R // 2)
        flight[j].wait_recv()
        flight[j] = send(5, j, land.at[here], land.at[here], j % 4)
        share(j, block_rows(0, j), R // 2)
    for j in range(STREAMS):
        prepare_landmarks(0, j)

    dots = (dots0, dots1)
    held = (held0, held1)
    tops = [None] * RING

    def inner(t, block):
        here = slice(block * BLOCK, (block + 1) * BLOCK)
        product = lax.dot_general(ll[here, :], xx[t], (((1,), (1,)), ((), ())), preferred_element_type=F32)
        both = lsq2[here, :]
        logits = product - jnp.concatenate([both, both], axis=1) - xsq2[t]
        dots[t % 2][here, :] = logits
        top = jnp.max(logits, axis=0, keepdims=True)
        tops[t] = top if tops[t] is None else jnp.maximum(tops[t], top)

    def outer(t, block, total, mass):
        here = slice(block * BLOCK, (block + 1) * BLOCK)
        weight = jnp.exp(dots[t % 2][here, :] - tops[t])
        hi, lo = split(weight)
        part = jnp.dot(ww[:, here], hi, preferred_element_type=F32)
        part = part[:C] + part[C:] + jnp.dot(ww[0:C, here], lo, preferred_element_type=F32)
        here_mass = jnp.sum(weight, axis=0, keepdims=True)
        if total is None:
            return part, here_mass
        return total + part, mass + here_mass

    def piece_rows(piece):
        return slice(0 if piece == 0 else HEAD + piece * PART, HEAD + (piece + 1) * PART)

    def ring_copy(t, side, piece):
        here = piece_rows(piece)
        here = pl.ds(here.start, here.stop - here.start)
        return pltpu.make_async_remote_copy(
            sent.at[t, side, here], got.at[t, side, here], ring_send.at[t, side, piece], ring_recv.at[t, side, piece],
            device_id=above if side == 0 else below, device_id_type=MESH,
        )

    scales = {}

    def handle(t, piece):
        mine_ref = held[t % 2]
        for side in range(2):
            lanes = slice(side * HALF, (side + 1) * HALF)
            if t > 0:
                ring_copy(t - 1, side, piece).wait_recv()
            if piece == 0:
                m, s = mine_ref[0:1, lanes], mine_ref[1:2, lanes]
                mine = theirs = None
                if t > 0:
                    m_in, s_in = got[t - 1, side, 0:1, :], got[t - 1, side, 1:2, :]
                    m_new = jnp.maximum(m, m_in)
                    mine, theirs = jnp.exp(m - m_new), jnp.exp(m_in - m_new)
                    m, s = m_new, s * mine + s_in * theirs
                if t < RING - 1:
                    sent[t, side, 0:HEAD, :] = jnp.concatenate([m, s, jnp.zeros((HEAD - 2, HALF), F32)], axis=0)
                scales[side] = mine, theirs, s
            mine, theirs, s = scales[side]
            rows = slice(HEAD + piece * PART, HEAD + (piece + 1) * PART)
            p = mine_ref[rows, lanes]
            if t > 0:
                p = p * mine + got[t - 1, side, rows, :] * theirs
            if t < RING - 1:
                sent[t, side, rows, :] = p
                ring_copy(t, side, piece).start()
            else:
                mine_ref[rows, lanes] = p / s

    for j in range(STREAMS):
        shares[j].wait_recv()
        prepare_landmarks(1, j)
    for t in range(2):
        for block in range(2):
            inner(t, block)
    for j in range(STREAMS):
        flight[j].wait_recv()
        share(STREAMS + j, block_rows(2, j), R // 2)
    for j in range(STREAMS):
        prepare_landmarks(2, j)
    inner(0, 2)
    for j in range(STREAMS):
        shares[STREAMS + j].wait_recv()
        prepare_landmarks(3, j)
    inner(0, 3)

    for t in range(RING):
        total = mass = None
        for block in range(BLOCKS):
            if t + 1 < RING and not (t == 0 and block < 2):
                inner(t + 1, block)
            total, mass = outer(t, block, total, mass)
            if t >= 2 and block < SUBS:
                handle(t - 1, block)
        held[t % 2][0:1, :] = tops[t]
        held[t % 2][1:2, :] = mass
        held[t % 2][HEAD:, :] = total
        if t == 0:
            for piece in range(SUBS):
                handle(0, piece)
    last = RING - 1
    for piece in range(SUBS):
        handle(last, piece)
        if (piece + 1) * PART % 128 == 0:
            done = (piece + 1) * PART
            out_ref[:, done - 128 : done] = held[last % 2][HEAD + done - 128 : HEAD + done, :].T

    for copy in copies + shares:
        copy.wait_send()
    for t in range(RING - 1):
        for side in range(2):
            for piece in range(SUBS):
                ring_copy(t, side, piece).wait_send()


def shards(embeddings, landmark_index, cluster_weights):
    vmem = lambda *shape, dtype=F32: pltpu.VMEM(shape, dtype)
    dma = lambda *shape: pltpu.SemaphoreType.DMA(shape)
    return pl.pallas_call(
        kernel,
        out_shape=jax.ShapeDtypeStruct((CHUNK, C), F32),
        in_specs=[
            pl.BlockSpec(memory_space=pl.ANY),
            pl.BlockSpec(memory_space=pltpu.SMEM),
            pl.BlockSpec(memory_space=pl.ANY),
        ],
        out_specs=pl.BlockSpec(memory_space=pltpu.VMEM),
        scratch_shapes=[
            vmem(ROWS, D),
            vmem(OWN, D),
            vmem(PAIR, D),
            vmem(STREAMS, R // 2, D),
            vmem(STREAMS, R // 4, D),
            vmem(STREAMS, R // 4, D),
            vmem(STREAMS, R // 4, D),
            vmem(STREAMS, R // 2, D),
            vmem(STREAMS, R // 4, D),
            vmem(STREAMS, R // 4, D),
            vmem(PAIR, C),
            vmem(2 * C, PAIR, dtype=BF16),
            vmem(PAIR, 3 * D, dtype=BF16),
            vmem(PAIR, 128),
            vmem(RING, CHUNK, 3 * D, dtype=BF16),
            vmem(RING, 1, CHUNK),
            vmem(PAIR, CHUNK),
            vmem(PAIR, CHUNK),
            vmem(MSG, CHUNK),
            vmem(MSG, CHUNK),
            vmem(RING - 1, 2, MSG, HALF),
            vmem(RING - 1, 2, MSG, HALF),
            dma(LOADS),
            pltpu.SemaphoreType.DMA,
            dma(6, STREAMS),
            dma(6, STREAMS),
            dma(2 * STREAMS),
            dma(2 * STREAMS),
            pltpu.SemaphoreType.DMA,
            pltpu.SemaphoreType.DMA,
            dma(RING - 1, 2, SUBS),
            dma(RING - 1, 2, SUBS),
        ],
        compiler_params=pltpu.CompilerParams(
            collective_id=0, has_side_effects=True, vmem_limit_bytes=56 * 2**20
        ),
    )(embeddings, landmark_index, cluster_weights)


def solution(mesh):
    return jax.shard_map(
        shards,
        mesh=mesh,
        in_specs=(P("sample", None), P("landmark"), P("landmark", None)),
        out_specs=P(("sample", "landmark"), None),
        check_vma=False,
    )
```

time: 76.7 us -> 70.5 us (0.919)
  the two profiles are of different devices: /device:TPU:64 before, /device:TPU:8 now
where the time goes in v3:
time: 70.5 us; the launch traced here: 70.3 us
  Pallas kernels  68.7 us (97%)
  local copies, waits for them, and re-layouts  1.67 us (2%)
    pallas_call x1, Pallas kernels, shards(): pl.pallas_call(kernel, out_shape=jax.ShapeDtypeStruct((CHUNK, C), F32), i...  68.7 us
    unnamed x1, local copies, waits for them, and re-layouts  1.67 us

profile of v3, /device:TPU:8, one launch (start us, length us, event | category | flops | bytes accessed | tf_op | source)
XLA Modules:
  0.0 70.3 jit_solution(10672145808993798704)
XLA Ops:
  0.0 68.7 %shard_map.37 = f32[256,256]{1,0:T(8,128)} custom-call(f32[4096,512]{1,0:T(8,128)} %emb_hbm.1, s32[512]{0:T(512)} %idx_ref.1, f32[512,256]{1,0:T(8,128)} %w_hbm.1), custom_call_target="tpu_custom_call" | custom-call | tf_op jit(solution)/shard_map/pallas_call | solution.py:316
  68.7 1.7 %copy.5 = f32[256,256]{1,0:T(8,128)} copy(f32[256,256]{1,0:T(8,128)} %shard_map.37) | data formatting | bytes 524288

commit v4 on v3

--- a/solution.py
+++ b/solution.py
@@ -21,11 +21,13 @@
 R = OWN // STREAMS
 HEAD = 8
 MSG = HEAD + C
-SUBS = 4
+SUBS = 2
 PART = C // SUBS
 BLOCKS = 4
 BLOCK = PAIR // BLOCKS
 LOADS = 8
+ORDER = (4, 3, -3, 2, -2, 1, -1, 0)
+UNITS = RING - 1
 
 
 def split(a):
@@ -36,7 +38,7 @@
 def kernel(
     emb_hbm, idx_ref, w_hbm, out_ref,
     emb, pick, land, buf0, buf1, buf2, buf3, acc1, acc2, acc3,
-    wts, ww, ll, lsq2, xx, xsq2, dots0, dots1, held0, held1, sent, got,
+    wts, ww, ll, lsq2, xx, xsq2, dots0, dots1, held, sent, got,
     load_sem, w_sem, send_sem, recv_sem, sib_send, sib_recv, ws_send, ws_recv, ring_send, ring_recv,
 ):
     sample = lax.axis_index("sample")
@@ -84,18 +86,15 @@
         lax.fori_loop(0, count // 16, some, 0)
 
     def prepare(t):
-        up = ((z + 2 * RING - 1 - t) % RING * 2 + core) * CHUNK
-        down = ((z + 1 + t) % RING * 2 + core) * CHUNK + HALF
-        for side, start in enumerate((up, down)):
-            rows = emb[pl.ds(pl.multiple_of(start, HALF), HALF), :]
-            hi, lo = split(4.0 * rows)
-            here = pl.ds(side * HALF, HALF)
-            xx[t, here, 0:D] = hi
-            xx[t, here, D : 2 * D] = lo
-            xx[t, here, 2 * D :] = hi
-            sq = rows * rows
-            sq = (sq[:, 0:128] + sq[:, 128:256]) + (sq[:, 256:384] + sq[:, 384:512])
-            xsq2[t, :, side * HALF : (side + 1) * HALF] = 2.0 * jnp.sum(sq.T, axis=0, keepdims=True)
+        chip = (z + RING + ORDER[t]) % RING
+        rows = emb[pl.ds(pl.multiple_of((chip * 2 + core) * CHUNK, CHUNK), CHUNK), :]
+        hi, lo = split(4.0 * rows)
+        xx[t, :, 0:D] = hi
+        xx[t, :, D : 2 * D] = lo
+        xx[t, :, 2 * D :] = hi
+        sq = rows * rows
+        sq = (sq[:, 0:128] + sq[:, 128:256]) + (sq[:, 256:384] + sq[:, 384:512])
+        xsq2[t] = 2.0 * jnp.sum(sq.T, axis=0, keepdims=True)
 
     base = core * OWN
     other_base = (1 - core) * OWN
@@ -136,51 +135,40 @@
         copies.append(copy)
         return copy
 
-    for load in loads:
-        load.wait()
-    for j in range(STREAMS):
-        pick_rows(j * R + (1 - bits[j % 4]) * (R // 2), R // 2)
-    for t in range(RING):
-        prepare(t)
-    w_load.wait()
-    prepare_weights(0)
-    prepare_weights(2)
-
-    pl.semaphore_wait(barrier, 7)
-    flight = []
-    for j in range(STREAMS):
+    groups = [range(g, g + 4) for g in range(0, STREAMS, 4)]
+    flight = [None] * STREAMS
+    shares = [None] * (2 * STREAMS)
+
+    def pick_half(j, half):
+        pick_rows(j * R + half * (R // 2), R // 2)
+
+    def halve_first(j):
         b0 = bits[j % 4]
-        flight.append(send(0, j, pick.at[rows_at(j * R + (1 - b0) * (R // 2), R // 2)], buf0.at[j], j % 4))
-    w_send = pltpu.make_async_remote_copy(
-        wts.at[own_w], wts.at[own_w], ws_send, ws_recv, device_id=sibling, device_id_type=MESH
-    )
-    w_send.start()
-    for j in range(STREAMS):
-        pick_rows(j * R + bits[j % 4] * (R // 2), R // 2)
-    for j in range(STREAMS):
+        flight[j] = send(0, j, pick.at[rows_at(j * R + (1 - b0) * (R // 2), R // 2)], buf0.at[j], j % 4)
+
+    def halve_second(j):
         b0, b1 = bits[j % 4], bits[(j + 1) % 4]
         flight[j].wait_recv()
         acc1[j] = pick[rows_at(j * R + b0 * (R // 2), R // 2), :] + buf0[j]
         flight[j] = send(1, j, acc1.at[j, rows_at((1 - b1) * (R // 4), R // 4)], buf1.at[j], (j + 1) % 4)
-    for j in range(STREAMS):
+
+    def exchange_first(j):
         b1 = bits[(j + 1) % 4]
         flight[j].wait_recv()
         acc2[j] = acc1[j, rows_at(b1 * (R // 4), R // 4), :] + buf1[j]
         flight[j] = send(2, j, acc2.at[j], buf2.at[j], (j + 2) % 4)
-    w_send.wait()
-    prepare_weights(1)
-    for j in range(STREAMS):
+
+    def exchange_second(j):
         flight[j].wait_recv()
         acc3[j] = acc2[j] + buf2[j]
         flight[j] = send(3, j, acc3.at[j], buf3.at[j], (j + 3) % 4)
-    prepare_weights(3)
-    for j in range(STREAMS):
+
+    def gather_first(j):
         b0, b1 = bits[j % 4], bits[(j + 1) % 4]
         here = rows_at(base + j * R + b0 * (R // 2) + b1 * (R // 4), R // 4)
         flight[j].wait_recv()
         land[here, :] = acc3[j] + buf3[j]
         flight[j] = send(4, j, land.at[here], land.at[here], (j + 1) % 4)
-    shares = []
 
     def share(which, start, count):
         here = rows_at(start, count)
@@ -189,18 +177,53 @@
             device_id=sibling, device_id_type=MESH,
         )
         copy.start()
-        shares.append(copy)
-
-    for j in range(STREAMS):
+        shares[which] = copy
+
+    def gather_second(j):
         here = rows_at(block_rows(0, j), R // 2)
         flight[j].wait_recv()
         flight[j] = send(5, j, land.at[here], land.at[here], j % 4)
         share(j, block_rows(0, j), R // 2)
+
+    def finish(j):
+        flight[j].wait_recv()
+        share(STREAMS + j, block_rows(2, j), R // 2)
+
+    for load in loads:
+        load.wait()
+    for g, group in enumerate(groups):
+        for j in group:
+            pick_half(j, 1 - bits[j % 4])
+        if g == 0:
+            pl.semaphore_wait(barrier, 7)
+        for j in group:
+            halve_first(j)
+        if g == 0:
+            prepare(0)
+            prepare(1)
+    w_load.wait()
+    w_send = pltpu.make_async_remote_copy(
+        wts.at[own_w], wts.at[own_w], ws_send, ws_recv, device_id=sibling, device_id_type=MESH
+    )
+    w_send.start()
+    for j in range(STREAMS):
+        pick_half(j, bits[j % 4])
+    fillers = [
+        lambda: (prepare(2), prepare(3), prepare(4), prepare(5)),
+        lambda: (prepare(6), prepare(7)),
+        lambda: (prepare_weights(0), prepare_weights(2)),
+        lambda: (w_send.wait_recv(), prepare_weights(1), prepare_weights(3)),
+    ]
+    for stage in (halve_second, exchange_first, exchange_second, gather_first, gather_second):
+        for group in groups:
+            for j in group:
+                stage(j)
+            if fillers:
+                fillers.pop(0)()
     for j in range(STREAMS):
         prepare_landmarks(0, j)
 
     dots = (dots0, dots1)
-    held = (held0, held1)
     tops = [None] * RING
 
     def inner(t, block):
@@ -226,43 +249,60 @@
     def piece_rows(piece):
         return slice(0 if piece == 0 else HEAD + piece * PART, HEAD + (piece + 1) * PART)
 
-    def ring_copy(t, side, piece):
+    def ring_copy(unit, side, piece):
         here = piece_rows(piece)
         here = pl.ds(here.start, here.stop - here.start)
         return pltpu.make_async_remote_copy(
-            sent.at[t, side, here], got.at[t, side, here], ring_send.at[t, side, piece], ring_recv.at[t, side, piece],
+            sent.at[unit, side, here], got.at[unit, side, here],
+            ring_send.at[unit, side, piece], ring_recv.at[unit, side, piece],
             device_id=above if side == 0 else below, device_id_type=MESH,
         )
 
+    def lanes_of(half):
+        return slice(half * HALF, (half + 1) * HALF)
+
     scales = {}
 
-    def handle(t, piece):
-        mine_ref = held[t % 2]
-        for side in range(2):
-            lanes = slice(side * HALF, (side + 1) * HALF)
-            if t > 0:
-                ring_copy(t - 1, side, piece).wait_recv()
-            if piece == 0:
-                m, s = mine_ref[0:1, lanes], mine_ref[1:2, lanes]
-                mine = theirs = None
-                if t > 0:
-                    m_in, s_in = got[t - 1, side, 0:1, :], got[t - 1, side, 1:2, :]
-                    m_new = jnp.maximum(m, m_in)
-                    mine, theirs = jnp.exp(m - m_new), jnp.exp(m_in - m_new)
-                    m, s = m_new, s * mine + s_in * theirs
-                if t < RING - 1:
-                    sent[t, side, 0:HEAD, :] = jnp.concatenate([m, s, jnp.zeros((HEAD - 2, HALF), F32)], axis=0)
-                scales[side] = mine, theirs, s
-            mine, theirs, s = scales[side]
-            rows = slice(HEAD + piece * PART, HEAD + (piece + 1) * PART)
-            p = mine_ref[rows, lanes]
-            if t > 0:
-                p = p * mine + got[t - 1, side, rows, :] * theirs
-            if t < RING - 1:
-                sent[t, side, rows, :] = p
-                ring_copy(t, side, piece).start()
-            else:
-                mine_ref[rows, lanes] = p / s
+    def merge(key, piece, chunk, half, incoming):
+        if piece == 0:
+            m, s = held[chunk, 0:1, lanes_of(half)], held[chunk, 1:2, lanes_of(half)]
+            factors = []
+            if incoming:
+                m_in = [got[u, side, 0:1, :] for u, side in incoming]
+                top = m
+                for other in m_in:
+                    top = jnp.maximum(top, other)
+                factors = [jnp.exp(other - top) for other in [m] + m_in]
+                s = s * factors[0]
+                for (u, side), factor in zip(incoming, factors[1:]):
+                    s = s + got[u, side, 1:2, :] * factor
+                m = top
+            scales[key] = factors, m, s
+        factors = scales[key][0]
+        rows = slice(HEAD + piece * PART, HEAD + (piece + 1) * PART)
+        p = held[chunk, rows, lanes_of(half)]
+        if incoming:
+            p = p * factors[0]
+            for (u, side), factor in zip(incoming, factors[1:]):
+                p = p + got[u, side, rows, :] * factor
+        return p
+
+    def handle(unit, sides=(0, 1)):
+        hop = (unit + 1) // 2
+        for piece in range(SUBS):
+            for side in sides:
+                incoming = []
+                if unit >= 2:
+                    ring_copy(unit - 2, side, piece).wait_recv()
+                    incoming = [(unit - 2, side)]
+                chunk = 0 if hop == 0 else 2 * hop - 1 + side
+                half = (unit + side) % 2
+                p = merge((unit, side), piece, chunk, half, incoming)
+                if piece == 0:
+                    m, s = scales[unit, side][1:]
+                    sent[unit, side, 0:HEAD, :] = jnp.concatenate([m, s, jnp.zeros((HEAD - 2, HALF), F32)], axis=0)
+                sent[unit, side, HEAD + piece * PART : HEAD + (piece + 1) * PART, :] = p
+                ring_copy(unit, side, piece).start()
 
     for j in range(STREAMS):
         shares[j].wait_recv()
@@ -270,11 +310,11 @@
     for t in range(2):
         for block in range(2):
             inner(t, block)
-    for j in range(STREAMS):
-        flight[j].wait_recv()
-        share(STREAMS + j, block_rows(2, j), R // 2)
-    for j in range(STREAMS):
-        prepare_landmarks(2, j)
+    for group in groups:
+        for j in group:
+            finish(j)
+        for j in group:
+            prepare_landmarks(2, j)
     inner(0, 2)
     for j in range(STREAMS):
         shares[STREAMS + j].wait_recv()
@@ -287,27 +327,37 @@
             if t + 1 < RING and not (t == 0 and block < 2):
                 inner(t + 1, block)
             total, mass = outer(t, block, total, mass)
-            if t >= 2 and block < SUBS:
-                handle(t - 1, block)
-        held[t % 2][0:1, :] = tops[t]
-        held[t % 2][1:2, :] = mass
-        held[t % 2][HEAD:, :] = total
+        held[t, 0:1, :] = tops[t]
+        held[t, 1:2, :] = mass
+        held[t, HEAD:, :] = total
         if t == 0:
-            for piece in range(SUBS):
-                handle(0, piece)
-    last = RING - 1
+            handle(0)
+        elif t == 1:
+            handle(1, (0,))
+        elif t == 2:
+            handle(1, (1,))
+        elif t == 4:
+            handle(2)
+        elif t == 6:
+            handle(3)
+    for unit in range(4, UNITS):
+        handle(unit)
     for piece in range(SUBS):
-        handle(last, piece)
-        if (piece + 1) * PART % 128 == 0:
-            done = (piece + 1) * PART
-            out_ref[:, done - 128 : done] = held[last % 2][HEAD + done - 128 : HEAD + done, :].T
-
+        for unit in (UNITS - 2, UNITS - 1):
+            for side in range(2):
+                ring_copy(unit, side, piece).wait_recv()
+        for half in range(2):
+            incoming = [(UNITS - 1 - half, 0), (UNITS - 2 + half, 1)]
+            p = merge(half, piece, RING - 1, half, incoming) / scales[half][2]
+            out_ref[lanes_of(half), piece * PART : (piece + 1) * PART] = p.T
+
+    w_send.wait_send()
     for copy in copies + shares:
         copy.wait_send()
-    for t in range(RING - 1):
+    for unit in range(UNITS):
         for side in range(2):
             for piece in range(SUBS):
-                ring_copy(t, side, piece).wait_send()
+                ring_copy(unit, side, piece).wait_send()
 
 
 def shards(embeddings, landmark_index, cluster_weights):
@@ -341,10 +391,9 @@
             vmem(RING, 1, CHUNK),
             vmem(PAIR, CHUNK),
             vmem(PAIR, CHUNK),
-            vmem(MSG, CHUNK),
-            vmem(MSG, CHUNK),
-            vmem(RING - 1, 2, MSG, HALF),
-            vmem(RING - 1, 2, MSG, HALF),
+            vmem(RING, MSG, CHUNK),
+            vmem(UNITS, 2, MSG, HALF),
+            vmem(UNITS, 2, MSG, HALF),
             dma(LOADS),
             pltpu.SemaphoreType.DMA,
             dma(6, STREAMS),
@@ -353,8 +402,8 @@
             dma(2 * STREAMS),
             pltpu.SemaphoreType.DMA,
             pltpu.SemaphoreType.DMA,
-            dma(RING - 1, 2, SUBS),
-            dma(RING - 1, 2, SUBS),
+            dma(UNITS, 2, SUBS),
+            dma(UNITS, 2, SUBS),
         ],
         compiler_params=pltpu.CompilerParams(
             collective_id=0, has_side_effects=True, vmem_limit_bytes=56 * 2**20

time: 70.5 us -> 66.1 us (0.938)
  the two profiles are of different devices: /device:TPU:8 before, /device:TPU:1 now
where the time goes in v4:
time: 66.1 us; the launch traced here: 66 us
  Pallas kernels  64.3 us (97%)
  local copies, waits for them, and re-layouts  1.67 us (3%)
    pallas_call x1, Pallas kernels, shards(): pl.pallas_call(kernel, out_shape=jax.ShapeDtypeStruct((CHUNK, C), F32), i...  64.3 us
    unnamed x1, local copies, waits for them, and re-layouts  1.67 us

profile of v4, /device:TPU:1, one launch (start us, length us, event | category | flops | bytes accessed | tf_op | source)
XLA Modules:
  0.0 66.0 jit_solution(17163413190871701874)
XLA Ops:
  0.0 64.3 %shard_map.37 = f32[256,256]{1,0:T(8,128)} custom-call(f32[4096,512]{1,0:T(8,128)} %emb_hbm.1, s32[512]{0:T(512)} %idx_ref.1, f32[512,256]{1,0:T(8,128)} %w_hbm.1), custom_call_target="tpu_custom_call" | custom-call | tf_op jit(solution)/shard_map/pallas_call | solution.py:366
  64.3 1.7 %copy.5 = f32[256,256]{1,0:T(8,128)} copy(f32[256,256]{1,0:T(8,128)} %shard_map.37) | data formatting | bytes 524288

commit v5 on v4

--- a/solution.py
+++ b/solution.py
@@ -57,10 +57,6 @@
     above = (sample, ((z + 1) % RING) * 2 + core)
     below = (sample, ((z + RING - 1) % RING) * 2 + core)
 
-    barrier = pltpu.get_barrier_semaphore()
-    for other in partners + [sibling, above, below]:
-        pl.semaphore_signal(barrier, inc=1, device_id=other, device_id_type=MESH)
-
     loads = []
     for i in range(LOADS):
         part = pl.ds(i * (ROWS // LOADS), ROWS // LOADS)
@@ -70,6 +66,10 @@
     own_w = pl.ds(pl.multiple_of(core * OWN, OWN), OWN)
     w_load = pltpu.make_async_copy(w_hbm, wts.at[own_w], w_sem)
     w_load.start()
+
+    barrier = pltpu.get_barrier_semaphore()
+    for other in partners + [sibling, above, below]:
+        pl.semaphore_signal(barrier, inc=1, device_id=other, device_id_type=MESH)
 
     first = sample * ROWS
 
@@ -235,9 +235,9 @@
         top = jnp.max(logits, axis=0, keepdims=True)
         tops[t] = top if tops[t] is None else jnp.maximum(tops[t], top)
 
-    def outer(t, block, total, mass):
+    def outer(t, block, total, mass, top):
         here = slice(block * BLOCK, (block + 1) * BLOCK)
-        weight = jnp.exp(dots[t % 2][here, :] - tops[t])
+        weight = jnp.exp(dots[t % 2][here, :] - top)
         hi, lo = split(weight)
         part = jnp.dot(ww[:, here], hi, preferred_element_type=F32)
         part = part[:C] + part[C:] + jnp.dot(ww[0:C, here], lo, preferred_element_type=F32)
@@ -245,6 +245,18 @@
         if total is None:
             return part, here_mass
         return total + part, mass + here_mass
+
+    def first_chunk(block, old):
+        inner(0, block)
+        if block == 0:
+            total, mass = outer(0, 0, None, None, tops[0])
+        else:
+            shrink = jnp.exp(old - tops[0])
+            total, mass = outer(0, block, held[0, HEAD:, :] * shrink, held[0, 1:2, :] * shrink, tops[0])
+        held[0, 0:1, :] = tops[0]
+        held[0, 1:2, :] = mass
+        held[0, HEAD:, :] = total
+        return tops[0]
 
     def piece_rows(piece):
         return slice(0 if piece == 0 else HEAD + piece * PART, HEAD + (piece + 1) * PART)
@@ -304,35 +316,37 @@
                 sent[unit, side, HEAD + piece * PART : HEAD + (piece + 1) * PART, :] = p
                 ring_copy(unit, side, piece).start()
 
+    top = first_chunk(0, None)
     for j in range(STREAMS):
         shares[j].wait_recv()
         prepare_landmarks(1, j)
-    for t in range(2):
-        for block in range(2):
-            inner(t, block)
+    top = first_chunk(1, top)
+    for block in range(2):
+        inner(1, block)
     for group in groups:
         for j in group:
             finish(j)
         for j in group:
             prepare_landmarks(2, j)
-    inner(0, 2)
+    top = first_chunk(2, top)
     for j in range(STREAMS):
         shares[STREAMS + j].wait_recv()
         prepare_landmarks(3, j)
-    inner(0, 3)
-
-    for t in range(RING):
+    first_chunk(3, top)
+    handle(0)
+    for block in range(2, BLOCKS):
+        inner(1, block)
+
+    for t in range(1, RING):
         total = mass = None
         for block in range(BLOCKS):
-            if t + 1 < RING and not (t == 0 and block < 2):
+            if t + 1 < RING:
                 inner(t + 1, block)
-            total, mass = outer(t, block, total, mass)
+            total, mass = outer(t, block, total, mass, tops[t])
         held[t, 0:1, :] = tops[t]
         held[t, 1:2, :] = mass
         held[t, HEAD:, :] = total
-        if t == 0:
-            handle(0)
-        elif t == 1:
+        if t == 1:
             handle(1, (0,))
         elif t == 2:
             handle(1, (1,))

time: 66.1 us -> 65.1 us (0.985)
  Pallas kernels: 64.3 us -> 63.3 us
    pallas_call x1, Pallas kernels: 64.3 us -> 63.3 us  [shards(): pl.pallas_call(kernel, out_shape=jax.ShapeDtypeStruct((CHUNK, C), F32), i...]
where the time goes in v5:
time: 65.1 us; the launch traced here: 64.9 us
  Pallas kernels  63.3 us (97%)
  local copies, waits for them, and re-layouts  1.67 us (3%)
    pallas_call x1, Pallas kernels, shards(): pl.pallas_call(kernel, out_shape=jax.ShapeDtypeStruct((CHUNK, C), F32), i...  63.3 us
    unnamed x1, local copies, waits for them, and re-layouts  1.67 us

profile of v5, /device:TPU:1, one launch (start us, length us, event | category | flops | bytes accessed | tf_op | source)
XLA Modules:
  0.0 64.9 jit_solution(15670069754398699389)
XLA Ops:
  0.0 63.3 %shard_map.37 = f32[256,256]{1,0:T(8,128)} custom-call(f32[4096,512]{1,0:T(8,128)} %emb_hbm.1, s32[512]{0:T(512)} %idx_ref.1, f32[512,256]{1,0:T(8,128)} %w_hbm.1), custom_call_target="tpu_custom_call" | custom-call | tf_op jit(solution)/shard_map/pallas_call | solution.py:380
  63.3 1.7 %copy.5 = f32[256,256]{1,0:T(8,128)} copy(f32[256,256]{1,0:T(8,128)} %shard_map.37) | data formatting | bytes 524288

commit v6 on v5

--- a/solution.py
+++ b/solution.py
@@ -75,15 +75,15 @@
 
     def pick_rows(start, count):
         def some(i, carry):
-            for u in range(16):
-                row = start + i * 16 + u
+            for u in range(32):
+                row = start + i * 32 + u
                 place = idx_ref[row] - first
                 owned = jnp.logical_and(place >= 0, place < ROWS)
                 found = emb[pl.ds(jnp.clip(place, 0, ROWS - 1), 1), :]
                 pick[pl.ds(row, 1), :] = jnp.where(owned, found, 0.0)
             return carry
 
-        lax.fori_loop(0, count // 16, some, 0)
+        lax.fori_loop(0, count // 32, some, 0)
 
     def prepare(t):
         chip = (z + RING + ORDER[t]) % RING
@@ -191,16 +191,10 @@
 
     for load in loads:
         load.wait()
-    for g, group in enumerate(groups):
-        for j in group:
-            pick_half(j, 1 - bits[j % 4])
-        if g == 0:
-            pl.semaphore_wait(barrier, 7)
-        for j in group:
-            halve_first(j)
-        if g == 0:
-            prepare(0)
-            prepare(1)
+    pl.semaphore_wait(barrier, 7)
+    for j in range(STREAMS):
+        pick_half(j, 1 - bits[j % 4])
+        halve_first(j)
     w_load.wait()
     w_send = pltpu.make_async_remote_copy(
         wts.at[own_w], wts.at[own_w], ws_send, ws_recv, device_id=sibling, device_id_type=MESH
@@ -209,7 +203,8 @@
     for j in range(STREAMS):
         pick_half(j, bits[j % 4])
     fillers = [
-        lambda: (prepare(2), prepare(3), prepare(4), prepare(5)),
+        lambda: (prepare(0), prepare(1), prepare(2)),
+        lambda: (prepare(3), prepare(4), prepare(5)),
         lambda: (prepare(6), prepare(7)),
         lambda: (prepare_weights(0), prepare_weights(2)),
         lambda: (w_send.wait_recv(), prepare_weights(1), prepare_weights(3)),
@@ -350,9 +345,9 @@
             handle(1, (0,))
         elif t == 2:
             handle(1, (1,))
-        elif t == 4:
+        elif t == 3:
             handle(2)
-        elif t == 6:
+        elif t == 5:
             handle(3)
     for unit in range(4, UNITS):
         handle(unit)

time: 65.1 us -> 64 us (0.983)
  Pallas kernels: 63.3 us -> 62.2 us
    pallas_call x1, Pallas kernels: 63.3 us -> 62.2 us  [shards(): pl.pallas_call(kernel, out_shape=jax.ShapeDtypeStruct((CHUNK, C), F32), i...]
where the time goes in v6:
time: 64 us; the launch traced here: 63.9 us
  Pallas kernels  62.2 us (97%)
  local copies, waits for them, and re-layouts  1.67 us (3%)
    pallas_call x1, Pallas kernels, shards(): pl.pallas_call(kernel, out_shape=jax.ShapeDtypeStruct((CHUNK, C), F32), i...  62.2 us
    unnamed x1, local copies, waits for them, and re-layouts  1.67 us

profile of v6, /device:TPU:1, one launch (start us, length us, event | category | flops | bytes accessed | tf_op | source)
XLA Modules:
  0.0 63.9 jit_solution(10952195447922394696)
XLA Ops:
  0.0 62.2 %shard_map.37 = f32[256,256]{1,0:T(8,128)} custom-call(f32[4096,512]{1,0:T(8,128)} %emb_hbm.1, s32[512]{0:T(512)} %idx_ref.1, f32[512,256]{1,0:T(8,128)} %w_hbm.1), custom_call_target="tpu_custom_call" | custom-call | tf_op jit(solution)/shard_map/pallas_call | solution.py:375
  62.2 1.7 %copy.5 = f32[256,256]{1,0:T(8,128)} copy(f32[256,256]{1,0:T(8,128)} %shard_map.37) | data formatting | bytes 524288

commit v7 on v6

--- a/solution.py
+++ b/solution.py
@@ -21,7 +21,7 @@
 R = OWN // STREAMS
 HEAD = 8
 MSG = HEAD + C
-SUBS = 2
+SUBS = 1
 PART = C // SUBS
 BLOCKS = 4
 BLOCK = PAIR // BLOCKS

time: 64 us -> 63.8 us (level)
  no operation moved by 1% of the time
where the time goes in v7:
time: 63.8 us; the launch traced here: 63.6 us
  Pallas kernels  61.9 us (97%)
  local copies, waits for them, and re-layouts  1.67 us (3%)
    pallas_call x1, Pallas kernels, shards(): pl.pallas_call(kernel, out_shape=jax.ShapeDtypeStruct((CHUNK, C), F32), i...  61.9 us
    unnamed x1, local copies, waits for them, and re-layouts  1.67 us

profile of v7, /device:TPU:1, one launch (start us, length us, event | category | flops | bytes accessed | tf_op | source)
XLA Modules:
  0.0 63.6 jit_solution(311786822107856661)
XLA Ops:
  0.0 61.9 %shard_map.37 = f32[256,256]{1,0:T(8,128)} custom-call(f32[4096,512]{1,0:T(8,128)} %emb_hbm.1, s32[512]{0:T(512)} %idx_ref.1, f32[512,256]{1,0:T(8,128)} %w_hbm.1), custom_call_target="tpu_custom_call" | custom-call | tf_op jit(solution)/shard_map/pallas_call | solution.py:375
  62.0 1.7 %copy.5 = f32[256,256]{1,0:T(8,128)} copy(f32[256,256]{1,0:T(8,128)} %shard_map.37) | data formatting | bytes 524288
